TPU v7x, 32 devices: a whole 2x2x4 slice. The times are simulated.
32 devices in a mesh: dp: 8 (over z, x), expert: 4 (over y, core).
Axes of the slice: x: 2, y: 2, z: 4, core: 2. Of those that a mesh axis runs over, the one named last changes fastest.
Arguments:
- tokens: bfloat16 [1024, 4096], P('dp'), may hold values from -6 to 6
- w_gate: bfloat16 [4, 4096, 8192], P('expert', None, 'dp'), may hold values from -0.09375 to 0.09375
- w_up: bfloat16 [4, 4096, 8192], P('expert', None, 'dp'), may hold values from -0.09375 to 0.09375
- w_down: bfloat16 [4, 8192, 4096], P('expert', 'dp'), may hold values from -0.0625 to 0.0625
- chosen: int32 [4, 8, 2], P(None, 'dp'), may hold values from 0 to 127, as said below
- counts: int32 [4, 8], P(None, 'dp'), may hold values from 0 to 2, as said below
- gate_codes: int32 [4, 8, 2], P(None, 'dp'), may hold values from 16384 to 65536
Outputs:
- combined: bfloat16 [1024, 4096], P('dp', 'expert')
Inputs may be any that keep to these rules, and one draw needn't show every extreme that they name: `chosen`: the 2 entries of one expert's block for one shard are distinct. `counts`: one expert has all 2 slots live in every token shard.
All inputs are finite; a program needn't handle non-finite values.
Results may differ from a plain program's by a relative error of at most 0.005.
Values may be sent and summed in bfloat16 or wider, within the bound.
A program may use at most 64 MiB of HBM per device.

v0:
```python
import jax
import jax.numpy as jnp
from jax import lax
from jax.sharding import PartitionSpec as P


def on_device(tokens, w_gate, w_up, w_down, chosen, counts, gate_codes):
    slot_count = chosen.shape[2]
    owner_index = lax.axis_index("expert")
    slot_ids = jnp.arange(slot_count, dtype=jnp.int32)
    live_all = (slot_ids[None, :] < counts).astype(jnp.float32)
    weights_all = gate_codes[:, 0, :].astype(jnp.float32) / 65536.0 * live_all
    own_picks = lax.dynamic_index_in_dim(chosen[:, 0, :], owner_index, 0, keepdims=False)
    own_weights = lax.dynamic_index_in_dim(weights_all, owner_index, 0, keepdims=False)
    own_live = lax.dynamic_index_in_dim(live_all, owner_index, 0, keepdims=False)
    picked = jnp.take(tokens, own_picks, axis=0) * own_live[:, None].astype(jnp.bfloat16)
    gate_w = w_gate[0]
    up_w = w_up[0]
    down_w = w_down[0]
    block_rows = lax.all_gather(picked, "dp", axis=0, tiled=True)
    gate_proj = jnp.dot(block_rows, gate_w, preferred_element_type=jnp.float32)
    up_proj = jnp.dot(block_rows, up_w, preferred_element_type=jnp.float32)
    hidden = (jax.nn.silu(gate_proj) * up_proj).astype(jnp.bfloat16)
    returned = lax.psum_scatter(
        jnp.dot(hidden, down_w, preferred_element_type=jnp.float32),
        "dp",
        scatter_dimension=0,
        tiled=True,
    )
    positions = jnp.arange(tokens.shape[0], dtype=jnp.int32)
    selector = (positions[:, None] == own_picks[None, :]).astype(jnp.float32) * own_weights[None, :]
    dense_rows = jnp.dot(selector, returned, precision=lax.Precision.HIGHEST)
    summed = lax.psum_scatter(dense_rows, "expert", scatter_dimension=1, tiled=True)
    return summed.astype(jnp.bfloat16)


def solution(mesh):
    placed = (
        P("dp", None),
        P("expert", None, "dp"),
        P("expert", None, "dp"),
        P("expert", "dp", None),
        P(None, "dp", None),
        P(None, "dp"),
        P(None, "dp", None),
    )
    return jax.shard_map(
        on_device, mesh=mesh, in_specs=placed, out_specs=P("dp", "expert"), check_vma=False
    )
```

profile of v0, /device:TPU:0, one launch (start us, length us, event | category | flops | bytes accessed | tf_op | source)
XLA Modules:
  0.0 170.0 jit_solution(18248886987663586076)
XLA Ops:
  6.5 0.0 copy-start
  6.5 0.0 all-reduce.3.cloned.1.call-start
  6.5 0.9 dynamic-slice_reduce_fusion.1
  7.5 0.7 fusion.26
  8.2 0.2 fusion.27
  8.4 0.0 copy-done
  8.4 0.6 gather_fusion
  9.0 0.1 multiply_bitcast_fusion
  9.0 32.3 %all-gather = bf16[8,2,4096]{2,1,0:T(2,128)(2,1)S(1)} all-gather(bf16[1,2,4096]{2,1,0:T(2,128)(2,1)S(1)} %multiply_bitcast_fusion), channel_id=1, replica_groups=mesh['dp'=8,'expert'=4] {'dp'}, dimensions={0}, use_global_device_ids=true | all-gather | bytes 147456 | tf_op jit(solution)/shard_map/all_gather | solution.py:20
  41.4 0.1 reshape.58
  41.4 4.6 %fusion.4 = f32[16,1024]{1,0:T(8,128)S(1)} fusion(bf16[16,4096]{1,0:T(8,128)(2,1)S(1)} %reshape.58, bf16[1,4096,1024]{2,1,0:T(8,128)(2,1)} %param.8), kind=kOutput, calls=%fused_computation.5 | convolution fusion | flops 134217728 | bytes 8585216 | tf_op jit(solution)/shard_map/dot_general | solution.py:21
  46.0 0.0 copy-start.3
  46.0 8.8 %fusion = f32[16,4096]{1,0:T(8,128)} fusion(bf16[1,1024,4096]{2,1,0:T(8,128)(2,1)} %param.10, bf16[16,4096]{1,0:T(8,128)(2,1)S(1)} %reshape.58, bf16[1,4096,1024]{2,1,0:T(8,128)(2,1)} %param.9, f32[16,1024]{1,0:T(8,128)S(1)} %fusion.4), kind=kOutput, calls=%fused_computation.1 | convolution fusion | flops 268533760 | bytes 17235968 | tf_op jit(solution)/shard_map/dot_general | solution.py:25
  54.8 0.0 all-reduce.3.cloned.1.call-update
  54.8 0.0 reduce-scatter.2.cloned.1.call-start
  54.9 0.0 copy-done.1
  54.9 0.2 dynamic-slice_reduce_fusion
  55.1 0.0 copy-done.3
  55.1 0.7 dynamic-slice.1
  56.5 70.0 %all-reduce.3.cloned.1.call-done = f32[16,4096]{1,0:T(8,128)} async-done(((f32[16,4096]{1,0:T(8,128)}), f32[16,4096]{1,0:T(8,128)}) %all-reduce.3.cloned.1.call-update) | async-done | bytes 262160
  126.5 4.0 %fusion.19 = f32[128,4096]{1,0:T(8,128)} fusion(f32[16,4096]{1,0:T(8,128)} %all-reduce.3.cloned.1.call-done, u32[]{:T(128)S(6)} %multiply.3, f32[2]{0:T(128)S(1)} %dynamic-slice_reduce_fusion, s32[2]{0:T(128)S(1)} %dynamic-slice_reduce_fusion.1), kind=kOutput, calls=%fused_computation.14 | convolution fusion | flops 12583424 | bytes 2129940 | tf_op jit(solution)/shard_map/dot_general | solution.py:32
  130.5 0.0 reduce-scatter.2.cloned.1.call-update
  130.5 30.9 %reduce-scatter.2.cloned.1.call-done = f32[128,1024]{1,0:T(8,128)} async-done(((f32[128,4096]{1,0:T(8,128)}), f32[128,1024]{1,0:T(8,128)}) %reduce-scatter.2.cloned.1.call-update) | async-done | bytes 524304 | tf_op jit(solution)/shard_map/reduce_scatter | solution.py:33
  161.4 1.8 %convert_element_type.30 = bf16[128,1024]{1,0:T(8,128)(2,1)} convert(f32[128,1024]{1,0:T(8,128)} %reduce-scatter.2.cloned.1.call-done) | non-fusion elementwise | flops 131072 | bytes 786432 | tf_op jit(solution)/shard_map/convert_element_type | solution.py:34
  (7 shorter events, 0.0 us)
Async XLA Ops:
  6.5 1.8 %copy-start = (bf16[128,4096]{1,0:T(8,128)(2,1)S(1)}, bf16[128,4096]{1,0:T(8,128)(2,1)}, u32[]{:S(2)}) copy-start(bf16[128,4096]{1,0:T(8,128)(2,1)} %param.7) | copy-start | bytes 3145732
  6.5 119.9 %all-reduce.3.cloned.1.call-start = ((), (), s32[]{:S(2)}) async-start(), calls=%async_computation.2 | async-start | bytes 524288
  46.0 8.9 %copy-start.1 = (s32[4,1,2]{0,2,1:T(2,128)S(1)}, s32[4,1,2]{0,2,1:T(2,128)}, u32[]{:S(2)}) copy-start(s32[4,1,2]{0,2,1:T(2,128)} %param.13) | copy-start | bytes 100
  46.0 8.9 %copy-start.2 = (s32[4,1]{0,1:T(1,128)S(1)}, s32[4,1]{0,1:T(1,128)}, u32[]{:S(2)}) copy-start(s32[4,1]{0,1:T(1,128)} %param.12) | copy-start | bytes 52
  46.0 9.1 %copy-start.3 = (u32[32]{0:T(128)S(1)}, u32[32]{0:T(128)}, u32[]{:S(2)}) copy-start(u32[32]{0:T(128)} %constant.49) | copy-start | bytes 388
  54.8 106.5 %reduce-scatter.2.cloned.1.call-start = ((), (), s32[]{:S(2)}) async-start(), calls=%async_computation.1 | async-start | bytes 2621440 | tf_op jit(solution)/shard_map/reduce_scatter | solution.py:33
Sparse Core Ops, SparseCore 0:
  55.0 71.4 all-reduce.2
  130.6 30.6 reduce-scatter.1
where the time goes:
time: 170 us
  waiting for transfers between devices  101 us (59%)
  blocking collectives  32.3 us (19%)
  matrix products  17.4 us (10%)
  between operations  14.2 us (8%)
  local copies, waits for them, and re-layouts  2.63 us (2%)
  other arithmetic  2.55 us (1%)
    unnamed x3, waiting for transfers between devices  70 us
    all_gather x1, blocking collectives, on_device(): block_rows = lax.all_gather(picked, 'dp', axis=0, tiled=True)  32.3 us
    reduce_scatter x1, waiting for transfers between devices, on_device(): lax.psum_scatter(dense_rows, 'expert', scatter_dimension=1, tiled=True)  30.9 us
    dot_general x1, matrix products, on_device(): jnp.dot(hidden, down_w, preferred_element_type=jnp.float32)  8.81 us
    dot_general x1, matrix products, on_device(): gate_proj = jnp.dot(block_rows, gate_w, preferred_element_type=jnp.float32)  4.57 us
    dot_general x1, matrix products, on_device(): dense_rows = jnp.dot(selector, returned, precision=lax.Precision.HIGHEST)  4.03 us
  transfers between devices with their start and end apart: 2, of which 2 were waited for; matrix products, arithmetic and copies ran while one was open for 1% of the time, Pallas kernels for 0%

commit v1 on v0

v1 whole, which is shorter than its diff:
```python
import functools

import jax
import jax.numpy as jnp
from jax import lax
from jax.experimental import pallas as pl
from jax.experimental.pallas import tpu as pltpu
from jax.sharding import PartitionSpec as P

LANES = 128
TILE = 16
MESH = pl.DeviceIdType.MESH


def iota(shape, dim):
    return lax.broadcasted_iota(jnp.int32, shape, dim)


def one_hot(hit):
    return jnp.where(hit, 1.0, 0.0).astype(jnp.bfloat16)


def matmul(a, b):
    return jnp.dot(a, b, preferred_element_type=jnp.float32)


def moe_kernel(
    n_dp, n_ex,
    chosen, counts, codes, tokens, w_gate, w_up, w_down, out,
    tok, wg, wu, wd, pick, gathered, lhs, gate, up, hidden, back_perm, ready, landed,
    tok_sem, wg_sem, wu_sem, wd_sem, pick_send, pick_recv, back_send, back_recv,
):
    n = n_dp * n_ex
    my_dp, my_ex = lax.axis_index("dp"), lax.axis_index("expert")
    me = my_dp * n_ex + my_ex
    slots = chosen.shape[2]
    rows = n_dp * slots
    per_row = TILE // slots
    depth = pick.shape[1]
    n_tok = tok.shape[0]
    width = wd.shape[2]
    pieces = width // LANES
    block = ready.shape[2]

    tok_copy = pltpu.make_async_copy(tokens, tok, tok_sem)
    tok_copy.start()

    def in_copies(k):
        part = pl.ds(k * depth, depth)
        return (
            pltpu.make_async_copy(w_gate.at[0, part, :], wg.at[k], wg_sem.at[k]),
            pltpu.make_async_copy(w_up.at[0, part, :], wu.at[k], wu_sem.at[k]),
        )

    def feature_block(i):
        return lax.rem(my_ex + 1 + i, n_ex)

    def down_copy(i):
        part = pl.ds(pl.multiple_of(feature_block(i) * width, LANES), width)
        return pltpu.make_async_copy(w_down.at[0, :, part], wd.at[i], wd_sem.at[i])

    @pl.loop(0, per_row)
    def _(k):
        for copy in in_copies(k):
            copy.start()

    @pl.loop(0, n_ex)
    def _(i):
        down_copy(i).start()

    barrier = pltpu.get_barrier_semaphore()

    @pl.loop(1, n)
    def _(k):
        other = lax.rem(me + k, n)
        pl.semaphore_signal(
            barrier, inc=1, device_id=(other // n_ex, lax.rem(other, n_ex)), device_id_type=MESH
        )

    row = iota((TILE, n_tok), 0)
    named = jnp.zeros((TILE, n_tok), jnp.int32)
    for j in range(slots):
        named = jnp.where(row // per_row == j, chosen[my_ex, 0, j], named)
    hit = named == iota((TILE, n_tok), 1)
    tok_copy.wait()
    picked = jnp.zeros((TILE, depth), jnp.float32)
    for k in range(per_row):
        select = one_hot(jnp.logical_and(hit, row % per_row == k))
        picked += matmul(select, tok[:, k * depth:(k + 1) * depth])
    pick[...] = picked.astype(jnp.bfloat16)

    pl.semaphore_wait(barrier, n - 1)

    @pl.loop(1, n_dp)
    def _(k):
        pltpu.make_async_remote_copy(
            src_ref=pick, dst_ref=gathered.at[my_dp],
            send_sem=pick_send, recv_sem=pick_recv,
            device_id=(lax.rem(my_dp + k, n_dp), my_ex), device_id_type=MESH,
        ).start()

    pltpu.make_async_copy(pick, gathered.at[my_dp], pick_recv).start()

    gate[...] = jnp.zeros_like(gate)
    up[...] = jnp.zeros_like(up)
    to = iota(back_perm.shape, 0)
    source = iota(back_perm.shape, 1)
    place = to % block
    back_perm[...] = one_hot(
        jnp.logical_and(
            source == (place % pieces) * rows + (to // block) * slots + place // pieces,
            place < slots * pieces,
        )
    )

    weight_rows = n_ex * block
    wrow = iota((weight_rows, LANES), 0)
    wslot = (wrow // block) * slots + (wrow % block) // pieces
    wvalid = wrow % block < slots * pieces
    weight = jnp.zeros((weight_rows, LANES), jnp.float32)
    column = iota((n_tok, weight_rows), 1)
    cslot = (column // block) * slots + (column % block) // pieces
    cvalid = column % block < slots * pieces
    token_of = jnp.full((n_tok, weight_rows), -1, jnp.int32)
    for e in range(n_ex):
        for j in range(slots):
            own = codes[e, 0, j].astype(jnp.float32) / 65536.0
            own = jnp.where(j < counts[e, 0], own, 0.0)
            weight = jnp.where(jnp.logical_and(wvalid, wslot == e * slots + j), own, weight)
            token_of = jnp.where(
                jnp.logical_and(cvalid, cslot == e * slots + j), chosen[e, 0, j], token_of
            )
    scatter = one_hot(token_of == iota((n_tok, weight_rows), 0))

    pltpu.make_async_copy(gathered, gathered, pick_recv).wait()

    stacked = gathered[...].reshape(n_dp * TILE, depth)
    to = iota((rows, n_dp * TILE), 0)
    source = iota((rows, n_dp * TILE), 1)
    first = (to // slots) * TILE + (to % slots) * per_row
    for k in range(per_row):
        lhs[k] = matmul(one_hot(source == first + k), stacked).astype(jnp.bfloat16)

    @pl.loop(0, per_row)
    def _(k):
        for copy in in_copies(k):
            copy.wait()
        gate[...] += matmul(lhs[k], wg[k])
        up[...] += matmul(lhs[k], wu[k])

    value = gate[...]
    hidden[...] = (value / (1.0 + jnp.exp(-value)) * up[...]).astype(jnp.bfloat16)

    @pl.loop(0, n_ex)
    def _(i):
        f = feature_block(i)
        down_copy(i).wait()
        part = matmul(hidden[...], wd[i]).astype(jnp.bfloat16)
        piled = jnp.concatenate(
            [part[:, c * LANES:(c + 1) * LANES] for c in range(pieces)], axis=0
        )
        ready[i] = matmul(back_perm[...], piled).astype(jnp.bfloat16).reshape(n_dp, block, LANES)

        @pl.loop(0, n_dp)
        def _(k):
            s = lax.rem(my_dp + 1 + k, n_dp)
            own = jnp.logical_and(s == my_dp, f == my_ex)

            @pl.when(jnp.logical_not(own))
            def _():
                pltpu.make_async_remote_copy(
                    src_ref=ready.at[i, s], dst_ref=landed.at[me],
                    send_sem=back_send, recv_sem=back_recv,
                    device_id=(s, f), device_id_type=MESH,
                ).start()

            @pl.when(own)
            def _():
                pltpu.make_async_copy(ready.at[i, s], landed.at[me], back_recv).start()

    pltpu.make_async_copy(landed, landed, back_recv).wait()

    def add(s, total):
        held = landed[pl.ds(s * n_ex, n_ex)].astype(jnp.float32)
        return total + held.reshape(weight_rows, LANES)

    total = lax.fori_loop(0, n_dp, add, jnp.zeros((weight_rows, LANES), jnp.float32), unroll=n_dp <= 8)
    total = total * weight
    high = total.astype(jnp.bfloat16)
    rest = total - high.astype(jnp.float32)
    low = rest.astype(jnp.bfloat16)
    spot = (wrow % block) % pieces
    for c in range(pieces):
        mine = spot == c
        result = matmul(scatter, jnp.where(mine, high.astype(jnp.float32), 0.0).astype(jnp.bfloat16))
        result += matmul(scatter, jnp.where(mine, low.astype(jnp.float32), 0.0).astype(jnp.bfloat16))
        out[:, c * LANES:(c + 1) * LANES] = result.astype(out.dtype)

    sent = gathered.at[pl.ds(0, n_dp - 1)]
    pltpu.make_async_copy(sent, sent, pick_send).wait()
    sent = landed.at[pl.ds(0, n - 1)]
    pltpu.make_async_copy(sent, sent, back_send).wait()


def on_device(n_dp, n_ex, tokens, w_gate, w_up, w_down, chosen, counts, gate_codes):
    n_tok, d = tokens.shape
    hidden_units = w_gate.shape[2]
    slots = chosen.shape[2]
    rows = n_dp * slots
    per_row = TILE // slots
    depth = d // per_row
    width = d // n_ex
    pieces = width // LANES
    block = -(-slots * pieces // TILE) * TILE
    n = n_dp * n_ex
    bf16, f32 = jnp.bfloat16, jnp.float32
    dma = pltpu.SemaphoreType.DMA
    hbm = pl.BlockSpec(memory_space=pl.ANY)
    smem = pl.BlockSpec(memory_space=pltpu.SMEM)
    return pl.pallas_call(
        functools.partial(moe_kernel, n_dp, n_ex),
        out_shape=jax.ShapeDtypeStruct((n_tok, width), bf16),
        in_specs=[smem] * 3 + [hbm] * 4,
        out_specs=pl.BlockSpec(memory_space=pltpu.VMEM),
        scratch_shapes=[
            pltpu.VMEM((n_tok, d), bf16),
            pltpu.VMEM((per_row, depth, hidden_units), bf16),
            pltpu.VMEM((per_row, depth, hidden_units), bf16),
            pltpu.VMEM((n_ex, hidden_units, width), bf16),
            pltpu.VMEM((TILE, depth), bf16),
            pltpu.VMEM((n_dp, TILE, depth), bf16),
            pltpu.VMEM((per_row, rows, depth), bf16),
            pltpu.VMEM((rows, hidden_units), f32),
            pltpu.VMEM((rows, hidden_units), f32),
            pltpu.VMEM((rows, hidden_units), bf16),
            pltpu.VMEM((n_dp * block, pieces * rows), bf16),
            pltpu.VMEM((n_ex, n_dp, block, LANES), bf16),
            pltpu.VMEM((n, block, LANES), bf16),
            dma,
            dma((per_row,)),
            dma((per_row,)),
            dma((n_ex,)),
            dma,
            dma,
            dma,
            dma,
        ],
        compiler_params=pltpu.CompilerParams(
            collective_id=0, has_side_effects=True, vmem_limit_bytes=48 * 1024 * 1024
        ),
        cost_estimate=pl.CostEstimate(
            flops=6 * rows * d * hidden_units,
            bytes_accessed=6 * d * hidden_units,
            transcendentals=rows * hidden_units,
        ),
    )(chosen, counts, gate_codes, tokens, w_gate, w_up, w_down)


def solution(mesh):
    placed = (
        P("dp", None),
        P("expert", None, "dp"),
        P("expert", None, "dp"),
        P("expert", "dp", None),
        P(None, "dp", None),
        P(None, "dp"),
        P(None, "dp", None),
    )
    return jax.shard_map(
        functools.partial(on_device, mesh.shape["dp"], mesh.shape["expert"]),
        mesh=mesh, in_specs=placed, out_specs=P("dp", "expert"), check_vma=False,
    )
```

time: 170 us -> 27.8 us (0.16)
  waiting for transfers between devices: 101 us -> 0 us
  blocking collectives: 32.3 us -> 0 us
  Pallas kernels: 0 us -> 23.4 us
  matrix products: 17.4 us -> 0 us
  between operations: 14.2 us -> 0.01 us
  other arithmetic: 2.55 us -> 0 us
    unnamed x3 -> x0, waiting for transfers between devices: 70 us -> none
    all_gather x1 -> x0, blocking collectives: 32.3 us -> none  [on_device(): block_rows = lax.all_gather(picked, 'dp', axis=0, tiled=True)]
    reduce_scatter x1 -> x0, waiting for transfers between devices: 30.9 us -> none  [on_device(): lax.psum_scatter(dense_rows, 'expert', scatter_dimension=1, tiled=True)]
    pallas_call x0 -> x1, Pallas kernels: none -> 23.4 us  [on_device(): pl.pallas_call(functools.partial(moe_kernel, n_dp, n_ex), out_shape=jax.S...]
    dot_general x3 -> x0, matrix products: 17.4 us -> none  [the longest x1 8.81 us: on_device(): jnp.dot(hidden, down_w, preferred_element_type=jnp.float32)]
    unnamed x10 -> x6, local copies, waits for them, and re-layouts: 0.73 us -> 4.2 us
    convert_element_type x2 -> x0, other arithmetic: 2.44 us -> none  [the longest x1 1.78 us: on_device(): return summed.astype(jnp.bfloat16)]
  transfers between devices with their start and end apart: 2 -> 0, of which waited for: 2 -> 0; matrix products, arithmetic and copies ran while one was open for 1% -> 0% of each run, Pallas kernels for 0% -> 0%
where the time goes in v1:
time: 27.8 us; the launch traced here: 27.7 us
  Pallas kernels  23.4 us (84%)
  local copies, waits for them, and re-layouts  4.2 us (15%)
    pallas_call x1, Pallas kernels, on_device(): pl.pallas_call(functools.partial(moe_kernel, n_dp, n_ex), out_shape=jax.S...  23.4 us
    unnamed x6, local copies, waits for them, and re-layouts  4.2 us

profile of v1, /device:TPU:0, one launch (start us, length us, event | category | flops | bytes accessed | tf_op | source)
XLA Modules:
  0.0 27.7 jit_solution(892268179677412249)
XLA Ops:
  0.0 0.8 %copy.8.chosen = s32[4,1,2]{2,1,0:T(1,128)S(1)} copy(s32[4,1,2]{0,2,1:T(2,128)} %param.11) | data formatting | bytes 64 | tf_op args[4]
  0.8 0.7 %copy.9.counts = s32[4,1]{1,0:T(4,128)S(1)} copy(s32[4,1]{0,1:T(1,128)} %param.12) | data formatting | bytes 32 | tf_op args[5]
  1.5 0.8 %copy.10.codes = s32[4,1,2]{2,1,0:T(1,128)S(1)} copy(s32[4,1,2]{0,2,1:T(2,128)} %param.13) | data formatting | bytes 64 | tf_op args[6]
  2.3 0.0 copy-start
  2.3 1.2 %copy-done = bf16[128,4096]{1,0:T(8,128)(2,1)S(1)} copy-done((bf16[128,4096]{1,0:T(8,128)(2,1)S(1)}, bf16[128,4096]{1,0:T(8,128)(2,1)}, u32[]{:S(2)}) %copy-start) | copy-done | bytes 1048600
  3.5 23.4 %shard_map.73 = bf16[128,1024]{1,0:T(8,128)(2,1)S(1)} custom-call(s32[4,1,2]{2,1,0:T(1,128)S(1)} %copy.8.chosen, s32[4,1]{1,0:T(4,128)S(1)} %copy.9.counts, s32[4,1,2]{2,1,0:T(1,128)S(1)} %copy.10.codes, bf16[128,4096]{1,0:T(8,128)(2,1)S(1)} %copy-done, bf16[1,4096,1024]{2,1,0:T(8,128)(2,1)} %w_gate.1, bf16[1,4096,1024]{2,1,0:T(8,128)(2,1)} %w_up.1, ...), custom_call_target="tpu_custom_call" | custom-call | flops 402653184 | bytes 25165824 | tf_op jit(solution)/shard_map/pallas_call | solution.py:220
  27.0 0.7 %copy.12 = bf16[128,1024]{1,0:T(8,128)(2,1)} copy(bf16[128,1024]{1,0:T(8,128)(2,1)S(1)} %shard_map.73) | data formatting | bytes 524288
Async XLA Ops:
  2.3 1.2 %copy-start = (bf16[128,4096]{1,0:T(8,128)(2,1)S(1)}, bf16[128,4096]{1,0:T(8,128)(2,1)}, u32[]{:S(2)}) copy-start(bf16[128,4096]{1,0:T(8,128)(2,1)} %tokens.1) | copy-start | bytes 3145732

commit v2 on v1

--- a/solution.py
+++ b/solution.py
@@ -26,17 +26,18 @@
 
 def moe_kernel(
     n_dp, n_ex,
-    chosen, counts, codes, tokens, w_gate, w_up, w_down, out,
-    tok, wg, wu, wd, pick, gathered, lhs, gate, up, hidden, back_perm, ready, landed,
-    tok_sem, wg_sem, wu_sem, wd_sem, pick_send, pick_recv, back_send, back_recv,
+    chosen_hbm, counts_hbm, codes_hbm, tokens, w_gate, w_up, w_down, out,
+    chosen, counts, codes, tok, wg, wu, wd, pick, gathered, lhs, gate, up, hidden, back_perm, ready, landed,
+    slot_sem, tok_sem, wg_sem, wu_sem, wd_sem, pick_send, pick_recv, back_send, back_recv,
 ):
     n = n_dp * n_ex
     my_dp, my_ex = lax.axis_index("dp"), lax.axis_index("expert")
     me = my_dp * n_ex + my_ex
-    slots = chosen.shape[2]
+    slots = chosen.shape[1]
     rows = n_dp * slots
     per_row = TILE // slots
-    depth = pick.shape[1]
+    half = pick.shape[2]
+    depth = wg.shape[1]
     n_tok = tok.shape[0]
     width = wd.shape[2]
     pieces = width // LANES
@@ -44,6 +45,23 @@
 
     tok_copy = pltpu.make_async_copy(tokens, tok, tok_sem)
     tok_copy.start()
+    slot_copies = [
+        pltpu.make_async_copy(source, target, slot_sem.at[i])
+        for i, (source, target) in enumerate(
+            ((chosen_hbm, chosen), (counts_hbm, counts), (codes_hbm, codes))
+        )
+    ]
+    for copy in slot_copies:
+        copy.start()
+
+    barrier = pltpu.get_barrier_semaphore()
+
+    @pl.loop(1, n)
+    def _(k):
+        other = lax.rem(me + k, n)
+        pl.semaphore_signal(
+            barrier, inc=1, device_id=(other // n_ex, lax.rem(other, n_ex)), device_id_type=MESH
+        )
 
     def in_copies(k):
         part = pl.ds(k * depth, depth)
@@ -68,38 +86,33 @@
     def _(i):
         down_copy(i).start()
 
-    barrier = pltpu.get_barrier_semaphore()
-
-    @pl.loop(1, n)
-    def _(k):
-        other = lax.rem(me + k, n)
-        pl.semaphore_signal(
-            barrier, inc=1, device_id=(other // n_ex, lax.rem(other, n_ex)), device_id_type=MESH
-        )
-
     row = iota((TILE, n_tok), 0)
     named = jnp.zeros((TILE, n_tok), jnp.int32)
+    slot_copies[0].wait()
     for j in range(slots):
-        named = jnp.where(row // per_row == j, chosen[my_ex, 0, j], named)
+        named = jnp.where(row // per_row == j, chosen[0, j, my_ex], named)
     hit = named == iota((TILE, n_tok), 1)
+    select = [one_hot(jnp.logical_and(hit, row % per_row == k)) for k in range(per_row)]
     tok_copy.wait()
-    picked = jnp.zeros((TILE, depth), jnp.float32)
-    for k in range(per_row):
-        select = one_hot(jnp.logical_and(hit, row % per_row == k))
-        picked += matmul(select, tok[:, k * depth:(k + 1) * depth])
-    pick[...] = picked.astype(jnp.bfloat16)
+    for h in range(2):
+        picked = jnp.zeros((TILE, half), jnp.float32)
+        for k in range(per_row):
+            start = (h * per_row + k) * half
+            picked += matmul(select[k], tok[:, start:start + half])
+        pick[h] = picked.astype(jnp.bfloat16)
 
     pl.semaphore_wait(barrier, n - 1)
 
-    @pl.loop(1, n_dp)
-    def _(k):
-        pltpu.make_async_remote_copy(
-            src_ref=pick, dst_ref=gathered.at[my_dp],
-            send_sem=pick_send, recv_sem=pick_recv,
-            device_id=(lax.rem(my_dp + k, n_dp), my_ex), device_id_type=MESH,
-        ).start()
-
-    pltpu.make_async_copy(pick, gathered.at[my_dp], pick_recv).start()
+    for h in range(2):
+        @pl.loop(1, n_dp)
+        def _(k):
+            pltpu.make_async_remote_copy(
+                src_ref=pick.at[h], dst_ref=gathered.at[h, my_dp],
+                send_sem=pick_send, recv_sem=pick_recv.at[h],
+                device_id=(lax.rem(my_dp + k, n_dp), my_ex), device_id_type=MESH,
+            ).start()
+
+        pltpu.make_async_copy(pick.at[h], gathered.at[h, my_dp], pick_recv.at[h]).start()
 
     gate[...] = jnp.zeros_like(gate)
     up[...] = jnp.zeros_like(up)
@@ -122,31 +135,37 @@
     cslot = (column // block) * slots + (column % block) // pieces
     cvalid = column % block < slots * pieces
     token_of = jnp.full((n_tok, weight_rows), -1, jnp.int32)
+    for copy in slot_copies[1:]:
+        copy.wait()
     for e in range(n_ex):
         for j in range(slots):
-            own = codes[e, 0, j].astype(jnp.float32) / 65536.0
-            own = jnp.where(j < counts[e, 0], own, 0.0)
+            own = codes[0, j, e].astype(jnp.float32) / 65536.0
+            own = jnp.where(j < counts[0, e], own, 0.0)
             weight = jnp.where(jnp.logical_and(wvalid, wslot == e * slots + j), own, weight)
             token_of = jnp.where(
-                jnp.logical_and(cvalid, cslot == e * slots + j), chosen[e, 0, j], token_of
+                jnp.logical_and(cvalid, cslot == e * slots + j), chosen[0, j, e], token_of
             )
     scatter = one_hot(token_of == iota((n_tok, weight_rows), 0))
 
-    pltpu.make_async_copy(gathered, gathered, pick_recv).wait()
-
-    stacked = gathered[...].reshape(n_dp * TILE, depth)
     to = iota((rows, n_dp * TILE), 0)
     source = iota((rows, n_dp * TILE), 1)
     first = (to // slots) * TILE + (to % slots) * per_row
-    for k in range(per_row):
-        lhs[k] = matmul(one_hot(source == first + k), stacked).astype(jnp.bfloat16)
-
-    @pl.loop(0, per_row)
-    def _(k):
-        for copy in in_copies(k):
-            copy.wait()
-        gate[...] += matmul(lhs[k], wg[k])
-        up[...] += matmul(lhs[k], wu[k])
+    spread = [one_hot(source == first + k) for k in range(per_row)]
+    for h in range(2):
+        pltpu.make_async_copy(gathered.at[h], gathered.at[h], pick_recv.at[h]).wait()
+        stacked = gathered[h].reshape(n_dp * TILE, half)
+        for k in range(per_row):
+            q = h * per_row + k
+            lhs[q // 2, :, (q % 2) * half:(q % 2 + 1) * half] = (
+                matmul(spread[k], stacked).astype(jnp.bfloat16)
+            )
+
+        @pl.loop(h * per_row // 2, (h + 1) * per_row // 2)
+        def _(k):
+            for copy in in_copies(k):
+                copy.wait()
+            gate[...] += matmul(lhs[k], wg[k])
+            up[...] += matmul(lhs[k], wu[k])
 
     value = gate[...]
     hidden[...] = (value / (1.0 + jnp.exp(-value)) * up[...]).astype(jnp.bfloat16)
@@ -196,7 +215,7 @@
         result += matmul(scatter, jnp.where(mine, low.astype(jnp.float32), 0.0).astype(jnp.bfloat16))
         out[:, c * LANES:(c + 1) * LANES] = result.astype(out.dtype)
 
-    sent = gathered.at[pl.ds(0, n_dp - 1)]
+    sent = gathered.at[:, pl.ds(0, n_dp - 1)]
     pltpu.make_async_copy(sent, sent, pick_send).wait()
     sent = landed.at[pl.ds(0, n - 1)]
     pltpu.make_async_copy(sent, sent, back_send).wait()
@@ -215,20 +234,22 @@
     n = n_dp * n_ex
     bf16, f32 = jnp.bfloat16, jnp.float32
     dma = pltpu.SemaphoreType.DMA
-    hbm = pl.BlockSpec(memory_space=pl.ANY)
-    smem = pl.BlockSpec(memory_space=pltpu.SMEM)
+    hbm = pl.BlockSpec(memory_space=pltpu.HBM)
     return pl.pallas_call(
         functools.partial(moe_kernel, n_dp, n_ex),
         out_shape=jax.ShapeDtypeStruct((n_tok, width), bf16),
-        in_specs=[smem] * 3 + [hbm] * 4,
+        in_specs=[hbm] * 7,
         out_specs=pl.BlockSpec(memory_space=pltpu.VMEM),
         scratch_shapes=[
+            pltpu.SMEM((1, slots, n_ex), jnp.int32),
+            pltpu.SMEM((1, n_ex), jnp.int32),
+            pltpu.SMEM((1, slots, n_ex), jnp.int32),
             pltpu.VMEM((n_tok, d), bf16),
             pltpu.VMEM((per_row, depth, hidden_units), bf16),
             pltpu.VMEM((per_row, depth, hidden_units), bf16),
             pltpu.VMEM((n_ex, hidden_units, width), bf16),
-            pltpu.VMEM((TILE, depth), bf16),
-            pltpu.VMEM((n_dp, TILE, depth), bf16),
+            pltpu.VMEM((2, TILE, depth // 2), bf16),
+            pltpu.VMEM((2, n_dp, TILE, depth // 2), bf16),
             pltpu.VMEM((per_row, rows, depth), bf16),
             pltpu.VMEM((rows, hidden_units), f32),
             pltpu.VMEM((rows, hidden_units), f32),
@@ -236,24 +257,25 @@
             pltpu.VMEM((n_dp * block, pieces * rows), bf16),
             pltpu.VMEM((n_ex, n_dp, block, LANES), bf16),
             pltpu.VMEM((n, block, LANES), bf16),
+            dma((3,)),
             dma,
             dma((per_row,)),
             dma((per_row,)),
             dma((n_ex,)),
             dma,
-            dma,
+            dma((2,)),
             dma,
             dma,
         ],
         compiler_params=pltpu.CompilerParams(
-            collective_id=0, has_side_effects=True, vmem_limit_bytes=48 * 1024 * 1024
+            collective_id=0, has_side_effects=True, vmem_limit_bytes=60 * 1024 * 1024
         ),
         cost_estimate=pl.CostEstimate(
             flops=6 * rows * d * hidden_units,
             bytes_accessed=6 * d * hidden_units,
             transcendentals=rows * hidden_units,
         ),
-    )(chosen, counts, gate_codes, tokens, w_gate, w_up, w_down)
+    )(chosen.transpose(1, 2, 0), counts.T, gate_codes.transpose(1, 2, 0), tokens, w_gate, w_up, w_down)
 
 
 def solution(mesh):

time: 27.8 us -> 24.7 us (0.89)
  local copies, waits for them, and re-layouts: 4.2 us -> 1.67 us
  Pallas kernels: 23.4 us -> 22.8 us
    unnamed x6 -> x1, local copies, waits for them, and re-layouts: 4.2 us -> 1.67 us
    pallas_call x1, Pallas kernels: 23.4 us -> 22.8 us  [on_device(): pl.pallas_call(functools.partial(moe_kernel, n_dp, n_ex), out_shape=jax.S...]
where the time goes in v2:
time: 24.7 us; the launch traced here: 24.5 us
  Pallas kernels  22.8 us (92%)
  local copies, waits for them, and re-layouts  1.67 us (7%)
    pallas_call x1, Pallas kernels, on_device(): pl.pallas_call(functools.partial(moe_kernel, n_dp, n_ex), out_shape=jax.S...  22.8 us
    unnamed x1, local copies, waits for them, and re-layouts  1.67 us

profile of v2, /device:TPU:0, one launch (start us, length us, event | category | flops | bytes accessed | tf_op | source)
XLA Modules:
  0.0 24.5 jit_solution(14478478091959565153)
XLA Ops:
  0.0 22.8 %shard_map.73 = bf16[128,1024]{1,0:T(8,128)(2,1)} custom-call(s32[1,2,4]{2,1,0:T(2,128)} %bitcast.3, s32[1,4]{1,0:T(1,128)} %bitcast.5, s32[1,2,4]{2,1,0:T(2,128)} %bitcast.4, bf16[128,4096]{1,0:T(8,128)(2,1)} %tokens.1, bf16[1,4096,1024]{2,1,0:T(8,128)(2,1)} %w_gate.1, bf16[1,4096,1024]{2,1,0:T(8,128)(2,1)} %w_up.1, bf16[1,1024,4096]{2,1,0:T(8,128)(2,1)} %w_down.1), custom_call_target="tpu_custom_call" | custom-call | flops 402653184 | bytes 25165824 | tf_op jit(solution)/shard_map/pallas_call | solution.py:238
  22.9 1.7 %copy.9 = bf16[128,1024]{1,0:T(8,128)(2,1)} copy(bf16[128,1024]{1,0:T(8,128)(2,1)} %shard_map.73) | data formatting | bytes 524288

commit v3 on v2

--- a/solution.py
+++ b/solution.py
@@ -28,7 +28,7 @@
     n_dp, n_ex,
     chosen_hbm, counts_hbm, codes_hbm, tokens, w_gate, w_up, w_down, out,
     chosen, counts, codes, tok, wg, wu, wd, pick, gathered, lhs, gate, up, hidden, back_perm, ready, landed,
-    slot_sem, tok_sem, wg_sem, wu_sem, wd_sem, pick_send, pick_recv, back_send, back_recv,
+    slot_sem, tok_sem, wg_sem, wu_sem, wd_sem, pick_send, pick_recv, back_send, back_recv, column_sem,
 ):
     n = n_dp * n_ex
     my_dp, my_ex = lax.axis_index("dp"), lax.axis_index("expert")
@@ -56,11 +56,16 @@
 
     barrier = pltpu.get_barrier_semaphore()
 
-    @pl.loop(1, n)
+    @pl.loop(1, n_dp)
     def _(k):
-        other = lax.rem(me + k, n)
         pl.semaphore_signal(
-            barrier, inc=1, device_id=(other // n_ex, lax.rem(other, n_ex)), device_id_type=MESH
+            barrier, inc=1, device_id=(lax.rem(my_dp + k, n_dp), my_ex), device_id_type=MESH
+        )
+
+    @pl.loop(1, n_ex)
+    def _(k):
+        pl.semaphore_signal(
+            barrier, inc=1, device_id=(my_dp, lax.rem(my_ex + k, n_ex)), device_id_type=MESH
         )
 
     def in_copies(k):
@@ -101,7 +106,7 @@
             picked += matmul(select[k], tok[:, start:start + half])
         pick[h] = picked.astype(jnp.bfloat16)
 
-    pl.semaphore_wait(barrier, n - 1)
+    pl.semaphore_wait(barrier, n_dp - 1 + n_ex - 1)
 
     for h in range(2):
         @pl.loop(1, n_dp)
@@ -113,6 +118,12 @@
             ).start()
 
         pltpu.make_async_copy(pick.at[h], gathered.at[h, my_dp], pick_recv.at[h]).start()
+
+    @pl.loop(1, n_ex)
+    def _(k):
+        pl.semaphore_signal(
+            column_sem, inc=1, device_id=(my_dp, lax.rem(my_ex + k, n_ex)), device_id_type=MESH
+        )
 
     gate[...] = jnp.zeros_like(gate)
     up[...] = jnp.zeros_like(up)
@@ -167,6 +178,7 @@
             gate[...] += matmul(lhs[k], wg[k])
             up[...] += matmul(lhs[k], wu[k])
 
+    pl.semaphore_wait(column_sem, n_ex - 1)
     value = gate[...]
     hidden[...] = (value / (1.0 + jnp.exp(-value)) * up[...]).astype(jnp.bfloat16)
 
@@ -266,6 +278,7 @@
             dma((2,)),
             dma,
             dma,
+            pltpu.SemaphoreType.REGULAR,
         ],
         compiler_params=pltpu.CompilerParams(
             collective_id=0, has_side_effects=True, vmem_limit_bytes=60 * 1024 * 1024

time: 24.7 us -> 23.3 us (0.943)
  Pallas kernels: 22.8 us -> 21.5 us
    pallas_call x1, Pallas kernels: 22.8 us -> 21.5 us  [on_device(): pl.pallas_call(functools.partial(moe_kernel, n_dp, n_ex), out_shape=jax.S...]
where the time goes in v3:
time: 23.3 us; the launch traced here: 23.1 us
  Pallas kernels  21.5 us (92%)
  local copies, waits for them, and re-layouts  1.67 us (7%)
    pallas_call x1, Pallas kernels, on_device(): pl.pallas_call(functools.partial(moe_kernel, n_dp, n_ex), out_shape=jax.S...  21.5 us
    unnamed x1, local copies, waits for them, and re-layouts  1.67 us

profile of v3, /device:TPU:0, one launch (start us, length us, event | category | flops | bytes accessed | tf_op | source)
XLA Modules:
  0.0 23.1 jit_solution(5508625268881036643)
XLA Ops:
  0.0 21.5 %shard_map.73 = bf16[128,1024]{1,0:T(8,128)(2,1)} custom-call(s32[1,2,4]{2,1,0:T(2,128)} %bitcast.3, s32[1,4]{1,0:T(1,128)} %bitcast.5, s32[1,2,4]{2,1,0:T(2,128)} %bitcast.4, bf16[128,4096]{1,0:T(8,128)(2,1)} %tokens.1, bf16[1,4096,1024]{2,1,0:T(8,128)(2,1)} %w_gate.1, bf16[1,4096,1024]{2,1,0:T(8,128)(2,1)} %w_up.1, bf16[1,1024,4096]{2,1,0:T(8,128)(2,1)} %w_down.1), custom_call_target="tpu_custom_call" | custom-call | flops 402653184 | bytes 25165824 | tf_op jit(solution)/shard_map/pallas_call | solution.py:250
  21.5 1.7 %copy.9 = bf16[128,1024]{1,0:T(8,128)(2,1)} copy(bf16[128,1024]{1,0:T(8,128)(2,1)} %shard_map.73) | data formatting | bytes 524288

commit v4 on v3

--- a/solution.py
+++ b/solution.py
@@ -9,6 +9,7 @@
 
 LANES = 128
 TILE = 16
+PARTS = 4
 MESH = pl.DeviceIdType.MESH
 
 
@@ -99,7 +100,7 @@
     hit = named == iota((TILE, n_tok), 1)
     select = [one_hot(jnp.logical_and(hit, row % per_row == k)) for k in range(per_row)]
     tok_copy.wait()
-    for h in range(2):
+    for h in range(PARTS):
         picked = jnp.zeros((TILE, half), jnp.float32)
         for k in range(per_row):
             start = (h * per_row + k) * half
@@ -108,7 +109,7 @@
 
     pl.semaphore_wait(barrier, n_dp - 1 + n_ex - 1)
 
-    for h in range(2):
+    for h in range(PARTS):
         @pl.loop(1, n_dp)
         def _(k):
             pltpu.make_async_remote_copy(
@@ -162,16 +163,16 @@
     source = iota((rows, n_dp * TILE), 1)
     first = (to // slots) * TILE + (to % slots) * per_row
     spread = [one_hot(source == first + k) for k in range(per_row)]
-    for h in range(2):
+    for h in range(PARTS):
         pltpu.make_async_copy(gathered.at[h], gathered.at[h], pick_recv.at[h]).wait()
         stacked = gathered[h].reshape(n_dp * TILE, half)
         for k in range(per_row):
             q = h * per_row + k
-            lhs[q // 2, :, (q % 2) * half:(q % 2 + 1) * half] = (
+            lhs[q // PARTS, :, (q % PARTS) * half:(q % PARTS + 1) * half] = (
                 matmul(spread[k], stacked).astype(jnp.bfloat16)
             )
 
-        @pl.loop(h * per_row // 2, (h + 1) * per_row // 2)
+        @pl.loop(h * per_row // PARTS, (h + 1) * per_row // PARTS)
         def _(k):
             for copy in in_copies(k):
                 copy.wait()
@@ -260,8 +261,8 @@
             pltpu.VMEM((per_row, depth, hidden_units), bf16),
             pltpu.VMEM((per_row, depth, hidden_units), bf16),
             pltpu.VMEM((n_ex, hidden_units, width), bf16),
-            pltpu.VMEM((2, TILE, depth // 2), bf16),
-            pltpu.VMEM((2, n_dp, TILE, depth // 2), bf16),
+            pltpu.VMEM((PARTS, TILE, depth // PARTS), bf16),
+            pltpu.VMEM((PARTS, n_dp, TILE, depth // PARTS), bf16),
             pltpu.VMEM((per_row, rows, depth), bf16),
             pltpu.VMEM((rows, hidden_units), f32),
             pltpu.VMEM((rows, hidden_units), f32),
@@ -275,7 +276,7 @@
             dma((per_row,)),
             dma((n_ex,)),
             dma,
-            dma((2,)),
+            dma((PARTS,)),
             dma,
             dma,
             pltpu.SemaphoreType.REGULAR,

time: 23.3 us -> 23.4 us (level)
  no operation moved by 1% of the time
where the time goes in v4:
time: 23.4 us; the launch traced here: 23.3 us
  Pallas kernels  21.6 us (92%)
  local copies, waits for them, and re-layouts  1.67 us (7%)
    pallas_call x1, Pallas kernels, on_device(): pl.pallas_call(functools.partial(moe_kernel, n_dp, n_ex), out_shape=jax.S...  21.6 us
    unnamed x1, local copies, waits for them, and re-layouts  1.67 us

profile of v4, /device:TPU:0, one launch (start us, length us, event | category | flops | bytes accessed | tf_op | source)
XLA Modules:
  0.0 23.3 jit_solution(12523559258064128353)
XLA Ops:
  0.0 21.6 %shard_map.73 = bf16[128,1024]{1,0:T(8,128)(2,1)} custom-call(s32[1,2,4]{2,1,0:T(2,128)} %bitcast.3, s32[1,4]{1,0:T(1,128)} %bitcast.5, s32[1,2,4]{2,1,0:T(2,128)} %bitcast.4, bf16[128,4096]{1,0:T(8,128)(2,1)} %tokens.1, bf16[1,4096,1024]{2,1,0:T(8,128)(2,1)} %w_gate.1, bf16[1,4096,1024]{2,1,0:T(8,128)(2,1)} %w_up.1, bf16[1,1024,4096]{2,1,0:T(8,128)(2,1)} %w_down.1), custom_call_target="tpu_custom_call" | custom-call | flops 402653184 | bytes 25165824 | tf_op jit(solution)/shard_map/pallas_call | solution.py:251
  21.6 1.7 %copy.9 = bf16[128,1024]{1,0:T(8,128)(2,1)} copy(bf16[128,1024]{1,0:T(8,128)(2,1)} %shard_map.73) | data formatting | bytes 524288
